TPU v7x, 256 devices: a whole 4x4x8 slice. The times are simulated.
256 devices in a mesh: cal: 64 (over z, y, core), gr: 4 (over x).
Axes of the slice: x: 4, y: 4, z: 8, core: 2. Of those that a mesh axis runs over, the one named last changes fastest.
Arguments:
- features: bfloat16 [131072, 4096], P('cal', 'gr'), may hold values from -6 to 6
- coef: bfloat16 [4096], P('gr'), may hold values from -0.09375 to 0.09375
- log_exposure: float32 [131072], P('cal'), may hold values from -0.7 to 0.7
- claims: float32 [131072], P('cal'), may hold values from 0 to 4
- cluster_id: int32 [131072], P('cal'), may hold values from 0 to 1023
- period: int32 [131072], P('cal'), may hold values from 0 to 127, as said below
- period_effect: float32 [128], replicated, may hold values from -0.5 to 0.5
Outputs:
- meat: float32 [4096, 4096], P('cal', 'gr')
Inputs may be any that keep to these rules, and one draw needn't show every extreme that they name: `period`: rows of index d of cal lie in periods d * 2 to (d + 1) * 2 - 1.
All inputs are finite; a program needn't handle non-finite values.
Results may differ from a plain program's by a relative error of at most 0.0044.
Values sent between devices are 32-bit elements; how exact they have to be, the bound alone decides.
A program may use at most 64 MiB of HBM per device.

v0:
```python
import jax
import jax.numpy as jnp
from jax import lax
from jax.sharding import PartitionSpec as P

CL_DEV = 16


def per_device(features, coef, log_exposure, claims, cluster_id, period, period_effect):
    rows_here = features.shape[0]
    width = features.shape[1]
    n_cal = lax.axis_size("cal")
    clusters = CL_DEV * n_cal
    local_lin = jnp.dot(features, coef, preferred_element_type=jnp.float32)
    linear = lax.psum(local_lin, "gr")
    periods = period_effect.shape[0]
    table = jnp.where(
        period[:, None] == jnp.arange(periods, dtype=jnp.int32)[None, :],
        period_effect[None, :],
        jnp.float32(0.0),
    )
    shift = jnp.sum(table, axis=1)
    resid = (claims - jnp.exp(linear + log_exposure + shift)).astype(jnp.bfloat16)
    block = min(512, rows_here)
    count = rows_here // block
    feats = features.reshape(count, block, width)
    res_b = resid.reshape(count, block)
    ids_b = cluster_id.reshape(count, block)
    cluster_range = jnp.arange(clusters, dtype=jnp.int32)

    def step(carry, item):
        feat_blk, res_blk, id_blk = item
        picks = jnp.where(
            id_blk[:, None] == cluster_range[None, :], res_blk[:, None], jnp.bfloat16(0.0)
        )
        term = lax.dot_general(
            picks, feat_blk, (((0,), (0,)), ((), ())), preferred_element_type=jnp.float32
        )
        return (carry + term, None)

    partial_scores, _ = lax.scan(
        step, jnp.zeros((clusters, width), jnp.float32), (feats, res_b, ids_b)
    )
    owned = lax.psum_scatter(partial_scores, "cal", scatter_dimension=0, tiled=True)
    full_scores = lax.all_gather(owned, "gr", axis=1, tiled=True)
    scale = jnp.float32(1.0) / jnp.float32(rows_here * n_cal)
    meat_block = lax.psum_scatter(
        lax.dot_general(
            full_scores,
            owned,
            (((0,), (0,)), ((), ())),
            precision=lax.Precision.HIGHEST,
            preferred_element_type=jnp.float32,
        ),
        "cal",
        scatter_dimension=0,
        tiled=True,
    )
    return meat_block * scale


def solution(mesh):
    placed = (P("cal", "gr"), P("gr"), P("cal"), P("cal"), P("cal"), P("cal"), P())
    return jax.shard_map(
        per_device, mesh=mesh, in_specs=placed, out_specs=P("cal", "gr"), check_vma=False
    )
```

profile of v0, /device:TPU:37, one launch (start us, length us, event | category | flops | bytes accessed | tf_op | source)
XLA Modules:
  0.0 409.0 jit_solution(18031180852784625165)
XLA Ops:
  6.5 0.0 copy-start
  6.5 0.0 copy-start.4
  6.5 0.0 copy-start.1
  6.5 0.0 copy-start.2
  6.5 0.0 copy-start.3
  6.5 0.0 reduce-scatter.3.cloned.1.call-start
  6.6 0.7 reshape.19
  7.3 3.4 fusion.11
  10.7 6.4 %psum.7 = f32[2048]{0:T(1024)S(1)} all-reduce(f32[2048]{0:T(1024)S(1)} %bitcast.16), channel_id=1, replica_groups=mesh['cal'=64,'gr'=4] {'gr'}, use_global_device_ids=true, to_apply=%region_0.0 | all-reduce | flops 2048 | bytes 16384 | tf_op jit(solution)/shard_map/psum | solution.py:15
  17.1 0.0 copy-done
  17.1 0.0 copy-done.4
  17.1 0.0 copy-done.1
  17.1 0.6 select_reduce_fusion
  17.7 0.0 copy-done.2
  17.8 0.0 copy-done.3
  17.8 22.3 %while.11 = (s32[]{:T(128)}, f32[1024,1024]{1,0:T(8,128)}, s32[4,512]{1,0:T(4,128)S(1)}, bf16[4,512]{1,0:T(4,128)(2,1)S(1)}, bf16[4,512,1024]{2,1,0:T(8,128)(2,1)}, /*index=5*/s32[]{:T(128)}, s32[]{:T(128)}) while((s32[]{:T(128)}, f32[1024,1024]{1,0:T(8,128)}, s32[4,512]{1,0:T(4,128)S(1)}, bf16[4,512]{1,0:T(4,128)(2,1)S(1)}, ...), condition=%wide.region_3.4_spmd.clone, body=%wide.region_2.3_spmd.clone.sunk | while | flops 1076887552 | bytes 9446507 | solution.py:41
  17.9 4.6 %select_add_fusion.2 = f32[1024,1024]{1,0:T(8,128)} fusion(f32[1024,1024]{1,0:T(8,128)} %get-tuple-element.107, pred[]{:T(512)S(6)} %compare.3, bf16[4,512,1024]{2,1,0:T(8,128)(2,1)} %get-tuple-element.117, s32[]{:T(128)S(6)} %copy.10, s32[512]{0:T(512)S(1)} %bitcast.15, bf16[512]{0:T(512)(128)(2,1)S(1)} %dynamic-slice_reduce_fusion.2), kind=kOutput, calls=%fused_computation.1.clone.1 | convolution fusion | flops 1076887552 | bytes 9440261 | tf_op jit(solution)/shard_map/while/body/eval_jaxpr/dot_general | solution.py:36
  22.5 5.9 %select_add_fusion.2 = f32[1024,1024]{1,0:T(8,128)} fusion(f32[1024,1024]{1,0:T(8,128)} %get-tuple-element.107, pred[]{:T(512)S(6)} %compare.3, bf16[4,512,1024]{2,1,0:T(8,128)(2,1)} %get-tuple-element.117, s32[]{:T(128)S(6)} %copy.10, s32[512]{0:T(512)S(1)} %bitcast.15, bf16[512]{0:T(512)(128)(2,1)S(1)} %dynamic-slice_reduce_fusion.2), kind=kOutput, calls=%fused_computation.1.clone.1 | convolution fusion | flops 1076887552 | bytes 9440261 | tf_op jit(solution)/shard_map/while/body/eval_jaxpr/dot_general | solution.py:36
  28.4 5.9 %select_add_fusion.2 = f32[1024,1024]{1,0:T(8,128)} fusion(f32[1024,1024]{1,0:T(8,128)} %get-tuple-element.107, pred[]{:T(512)S(6)} %compare.3, bf16[4,512,1024]{2,1,0:T(8,128)(2,1)} %get-tuple-element.117, s32[]{:T(128)S(6)} %copy.10, s32[512]{0:T(512)S(1)} %bitcast.15, bf16[512]{0:T(512)(128)(2,1)S(1)} %dynamic-slice_reduce_fusion.2), kind=kOutput, calls=%fused_computation.1.clone.1 | convolution fusion | flops 1076887552 | bytes 9440261 | tf_op jit(solution)/shard_map/while/body/eval_jaxpr/dot_general | solution.py:36
  34.3 5.9 %select_add_fusion.2 = f32[1024,1024]{1,0:T(8,128)} fusion(f32[1024,1024]{1,0:T(8,128)} %get-tuple-element.107, pred[]{:T(512)S(6)} %compare.3, bf16[4,512,1024]{2,1,0:T(8,128)(2,1)} %get-tuple-element.117, s32[]{:T(128)S(6)} %copy.10, s32[512]{0:T(512)S(1)} %bitcast.15, bf16[512]{0:T(512)(128)(2,1)S(1)} %dynamic-slice_reduce_fusion.2), kind=kOutput, calls=%fused_computation.1.clone.1 | convolution fusion | flops 1076887552 | bytes 9440261 | tf_op jit(solution)/shard_map/while/body/eval_jaxpr/dot_general | solution.py:36
  40.1 0.0 reduce-scatter.3.cloned.1.call-update
  40.1 0.0 reduce-scatter.5.cloned.1.call-start
  40.2 142.6 %reduce-scatter.3.cloned.1.call-done = f32[16,1024]{1,0:T(8,128)} async-done(((f32[1024,1024]{1,0:T(8,128)}), f32[16,1024]{1,0:T(8,128)}) %reduce-scatter.3.cloned.1.call-update) | async-done | bytes 65552 | tf_op jit(solution)/shard_map/reduce_scatter | solution.py:44
  182.8 8.4 %all_gather.3 = f32[16,4096]{1,0:T(8,128)S(1)} all-gather(f32[16,1024]{1,0:T(8,128)} %reduce-scatter.3.cloned.1.call-done), channel_id=1, replica_groups=mesh['cal'=64,'gr'=4] {'gr'}, dimensions={1}, use_global_device_ids=true | all-gather | bytes 327680 | tf_op jit(solution)/shard_map/all_gather | solution.py:45
  191.1 16.7 %fusion.12 = f32[4096,1024]{1,0:T(8,128)} fusion(f32[16,4096]{1,0:T(8,128)S(1)} %all_gather.3, f32[16,1024]{1,0:T(8,128)} %reduce-scatter.3.cloned.1.call-done), kind=kOutput, calls=%fused_computation.18 | convolution fusion | flops 805306368 | bytes 17104896 | tf_op jit(solution)/shard_map/dot_general | solution.py:48
  207.8 0.0 reduce-scatter.5.cloned.1.call-update
  207.9 192.6 %reduce-scatter.5.cloned.1.call-done = f32[64,1024]{1,0:T(8,128)} async-done(((f32[4096,1024]{1,0:T(8,128)}), f32[64,1024]{1,0:T(8,128)}) %reduce-scatter.5.cloned.1.call-update) | async-done | bytes 262160 | tf_op jit(solution)/shard_map/reduce_scatter | solution.py:47
  400.5 1.7 broadcast_multiply_fusion
  (12 shorter events, 0.2 us)
Async XLA Ops:
  6.5 10.5 %copy-start = (s32[2048]{0:T(1024)S(1)}, s32[2048]{0:T(1024)}, u32[]{:S(2)}) copy-start(s32[2048]{0:T(1024)} %param.13) | copy-start | bytes 24580
  6.5 10.6 %copy-start.4 = (f32[128]{0:T(128)S(1)}, f32[128]{0:T(128)}, u32[]{:S(2)}) copy-start(f32[128]{0:T(128)} %param.15) | copy-start | bytes 1540
  6.5 10.6 %copy-start.1 = (s32[2048]{0:T(1024)S(1)}, s32[2048]{0:T(1024)}, u32[]{:S(2)}) copy-start(s32[2048]{0:T(1024)} %param.14) | copy-start | bytes 24580
  6.5 11.2 %copy-start.2 = (f32[2048]{0:T(1024)S(1)}, f32[2048]{0:T(1024)}, u32[]{:S(2)}) copy-start(f32[2048]{0:T(1024)} %param.12) | copy-start | bytes 24580
  6.5 11.2 %copy-start.3 = (f32[2048]{0:T(1024)S(1)}, f32[2048]{0:T(1024)}, u32[]{:S(2)}) copy-start(f32[2048]{0:T(1024)} %param.11) | copy-start | bytes 24580
  6.5 176.2 %reduce-scatter.3.cloned.1.call-start = ((), (), s32[]{:S(2)}) async-start(), calls=%async_computation.2 | async-start | bytes 4259840 | tf_op jit(solution)/shard_map/reduce_scatter | solution.py:44
  40.1 360.4 %reduce-scatter.5.cloned.1.call-start = ((), (), s32[]{:S(2)}) async-start(), calls=%async_computation.3 | async-start | bytes 17039360 | tf_op jit(solution)/shard_map/reduce_scatter | solution.py:47
Sparse Core Ops, SparseCore 0:
  40.3 142.4 reduce-scatter.2
  208.0 192.4 reduce-scatter.4
where the time goes:
time: 415 us; the launch traced here: 409 us
  waiting for transfers between devices  335 us (81%)
  matrix products  42.2 us (10%)
  blocking collectives  14.8 us (4%)
  between operations  13.5 us (3%)
    reduce_scatter x1, waiting for transfers between devices, per_device(): lax.psum_scatter(lax.dot_general(full_scores, owned, (((0,), (0,)), ((),...  193 us
    reduce_scatter x1, waiting for transfers between devices, per_device(): lax.psum_scatter(partial_scores, 'cal', scatter_dimension=0, tiled=True)  143 us
    dot_general x4, matrix products, step(): lax.dot_general(picks, feat_blk, (((0,), (0,)), ((), ())), preferred_elem...  22.2 us
    dot_general x1, matrix products, per_device(): lax.dot_general(full_scores, owned, (((0,), (0,)), ((), ())), precision=l...  16.7 us
    all_gather x1, blocking collectives, per_device(): full_scores = lax.all_gather(owned, 'gr', axis=1, tiled=True)  8.36 us
  transfers between devices with their start and end apart: 2, of which 2 were waited for; matrix products, arithmetic and copies ran while one was open for 0% of the time, Pallas kernels for 0%

commit v1 on v0

v1 whole, which is shorter than its diff:
```python
import jax
import jax.numpy as jnp
from jax import lax
from jax.experimental import pallas as pl
from jax.experimental.pallas import tpu as pltpu
from jax.sharding import PartitionSpec as P

NZ, NY, NX = 8, 4, 4
ROWS = 2048
WIDTH = 1024
HALF = 512
FCH = 4
TILES = 4
F32 = jnp.float32
BF16 = jnp.bfloat16


def remote(src, dst, send, recv, cal, gr):
    return pltpu.make_async_remote_copy(
        src_ref=src,
        dst_ref=dst,
        send_sem=send,
        recv_sem=recv,
        device_id=(cal, gr),
        device_id_type=pl.DeviceIdType.MESH,
    )


def split(v):
    hi = v.astype(BF16)
    lo = (v - hi.astype(F32)).astype(BF16)
    return hi, lo


def kernel(
    feat_hbm, coef_ref, logexp_ref, claims_ref, ids_ref, period_ref, effect_ref, out_ref,
    feat, cbuf, lin, res, picks, theirs, mine, core_rx, rx1, rx2, full, left, mpart, mrx,
    feat_sem, lin_send, lin_recv, core_send, core_recv,
    r1s, r1r, r2s, r2r, g1s, g1r, g2s, g2r, fws, fwr, m_send, m_recv,
):
    c = lax.axis_index("cal")
    x = lax.axis_index("gr")
    core = lax.rem(c, 2)
    y = lax.rem(lax.div(c, 2), NY)
    z = lax.div(c, 2 * NY)
    sib = c + 1 - 2 * core

    def cal_of(zz, yy):
        return (zz * NY + yy) * 2 + core

    fetches = []
    fr = ROWS // FCH
    for k in range(FCH):
        f = pltpu.make_async_copy(
            feat_hbm.at[pl.ds(k * fr, fr)], feat.at[pl.ds(k * fr, fr)], feat_sem.at[k]
        )
        f.start()
        fetches.append(f)

    barrier = pltpu.get_barrier_semaphore()
    peers = [(sib, x)]
    peers += [(c, lax.rem(x + k, NX)) for k in range(1, NX)]
    peers += [(cal_of(z, lax.rem(y + k, NY)), x) for k in (1, NY - 1)]
    peers += [(cal_of(lax.rem(z + k, NZ), y), x) for k in (1, NZ - 1)]
    for cal, gr in peers:
        pl.semaphore_signal(
            barrier, inc=1, device_id=(cal, gr), device_id_type=pl.DeviceIdType.MESH
        )

    cf = coef_ref[...].astype(F32)
    for j in range(WIDTH // 128):
        cbuf[:, j * 128 : (j + 1) * 128] = jnp.broadcast_to(cf[j : j + 1, :], (16, 128)).astype(BF16)
    for k in range(FCH):
        fetches[k].wait()
        part = lax.dot_general(
            cbuf[...], feat[k * fr : (k + 1) * fr, :], (((1,), (1,)), ((), ())),
            preferred_element_type=F32,
        )
        for j in range(fr // 128):
            lin[x, k * (fr // 128) + j, :] = part[0, j * 128 : (j + 1) * 128]
    pl.semaphore_wait(barrier, len(peers))

    sends = []
    for k in range(1, NX):
        s = remote(lin.at[x], lin.at[x], lin_send.at[k - 1], lin_recv.at[k - 1], c, lax.rem(x + k, NX))
        s.start()
        sends.append(s)
    eff = effect_ref[...]
    where = lax.broadcasted_iota(jnp.int32, (1, 128), 1)
    d = c * 2
    e0 = jnp.sum(jnp.where(where == d, eff, 0.0), axis=1, keepdims=True)
    e1 = jnp.sum(jnp.where(where == d + 1, eff, 0.0), axis=1, keepdims=True)
    per = period_ref[...]
    shift = jnp.where(per == d, e0, jnp.where(per == d + 1, e1, 0.0))
    for k in range(1, NX):
        src = lax.rem(x + NX - k, NX)
        remote(lin.at[src], lin.at[src], lin_send.at[k - 1], lin_recv.at[k - 1], c, x).wait_recv()
    linear = lin[0] + lin[1] + lin[2] + lin[3]
    value = claims_ref[...] - jnp.exp(linear + logexp_ref[...] + shift)
    res[...] = value.astype(BF16).astype(F32)

    def scores(base, dst, after):
        def build(j, carry):
            row = lax.broadcasted_iota(jnp.int32, (HALF, 128), 0) + base
            hit = row == ids_ref[pl.ds(j, 1), :]
            col = pl.ds(pl.multiple_of(j * 128, 128), 128)
            picks[:, col] = jnp.where(hit, res[pl.ds(j, 1), :], 0.0).astype(BF16)
            return carry

        lax.fori_loop(0, ROWS // 128, build, 0)
        w = WIDTH // TILES
        for n in range(TILES):
            dst[:, n * w : (n + 1) * w] = jnp.dot(
                picks[...], feat[:, n * w : (n + 1) * w], preferred_element_type=F32
            )
            after(n, pl.ds(n * w, w))

    def push(n, cols):
        s = remote(theirs.at[:, cols], core_rx.at[:, cols], core_send.at[n], core_recv.at[n], sib, x)
        s.start()
        sends.append(s)

    scores((1 - core) * HALF, theirs, push)

    def fold(n, cols):
        remote(theirs.at[:, cols], core_rx.at[:, cols], core_send.at[n], core_recv.at[n], sib, x).wait_recv()
        w = WIDTH // TILES
        mine[:, n * w : (n + 1) * w] += core_rx[:, n * w : (n + 1) * w]

    scores(core * HALF, mine, fold)
    for s in sends:
        s.wait_send()

    owner_x = lax.div(z, 2)
    lcol = pl.multiple_of((lax.rem(z, 2) * NY + y) * 128, 128)

    def plane(first, second):
        (n1, p1, dev1), (n2, p2, dev2) = first, second
        b1 = HALF // n1
        b2 = b1 // n2

        def reduce_ring(n, p, dev, base, rows, rx, ss, rs):
            h = n // 2
            started = []
            slot = [0] + [rows // 2 + i * rows for i in range(h - 1)]
            for s in range(h):
                dist = h - s
                for w in (0, 1):
                    step = n - dist if w == 0 else dist
                    target = base + lax.rem(p + step, n) * rows
                    size = rows
                    if s == 0:
                        size = rows // 2
                        target = target + w * size
                    target = pl.multiple_of(target, 8)
                    if s > 0:
                        prev = rows // 2 if s == 1 else rows
                        got = rx.at[w, pl.ds(slot[s - 1], prev)]
                        remote(got, got, ss.at[w, s - 1], rs.at[w, s - 1], c, x).wait_recv()
                        at = target + (w * prev if s == 1 else 0)
                        at = pl.ds(pl.multiple_of(at, 8), prev)
                        mine[at, :] += got[...]
                    to = dev(lax.rem(p + (n - 1 if w == 0 else 1), n))
                    cp = remote(
                        mine.at[pl.ds(target, size)], rx.at[w, pl.ds(slot[s], size)],
                        ss.at[w, s], rs.at[w, s], to, x,
                    )
                    cp.start()
                    started.append(cp)
            own = pl.ds(pl.multiple_of(base + p * rows, 8), rows)
            for w in (0, 1):
                got = rx.at[w, pl.ds(slot[h - 1], rows)]
                remote(got, got, ss.at[w, h - 1], rs.at[w, h - 1], c, x).wait_recv()
                mine[own, :] += got[...]
            return started

        def gather_ring(n, p, dev, base, rows, ss, rs, arrived):
            h = n // 2
            started = []
            for s in range(h + 1):
                for w in (0, 1):
                    if s > 0:
                        step = s if w == 0 else n - s
                        size = rows if s < h else rows // 2
                        start = base + lax.rem(p + step, n) * rows
                        if s == h:
                            start = start + w * size
                        got = full.at[pl.ds(pl.multiple_of(start, 8), size)]
                        remote(got, got, ss.at[w, s - 1], rs.at[w, s - 1], c, x).wait_recv()
                    if s < h:
                        step = s if w == 0 else lax.rem(n - s, n)
                        size = rows if s < h - 1 else rows // 2
                        start = base + lax.rem(p + step, n) * rows
                        if s == h - 1:
                            start = start + w * size
                        blk = full.at[pl.ds(pl.multiple_of(start, 8), size)]
                        to = dev(lax.rem(p + (n - 1 if w == 0 else 1), n))
                        cp = remote(blk, blk, ss.at[w, s], rs.at[w, s], to, x)
                        cp.start()
                        started.append(cp)
                if s > 0:
                    arrived(s)
            return started

        started = reduce_ring(n1, p1, dev1, 0, b1, rx1, r1s, r1r)
        base = p1 * b1
        started += reduce_ring(n2, p2, dev2, base, b2, rx2, r2s, r2r)
        own = pl.ds(pl.multiple_of(base + p2 * b2, 8), b2)
        full[own, :] = mine[own, :]
        started += gather_ring(n2, p2, dev2, base, b2, g2s, g2r, lambda s: None)

        def forward(event, block, go):
            at = pl.ds(pl.multiple_of(block * b1, 8), b1)
            src = full.at[at, pl.ds(lcol, 128)]
            for k in range(1, NX):
                to = lax.rem(x + k, NX)
                cp = remote(src, left.at[at], fws.at[event, k - 1], fwr.at[event], c, to)
                if go == "start":
                    cp.start()
                else:
                    cp.wait_send()

        def blocks_of(s):
            if s == 0:
                return [(0, p1)]
            if s == n1 // 2:
                return [(n1 - 1, lax.rem(p1 + s, n1))]
            return [(2 * s - 1, lax.rem(p1 + s, n1)), (2 * s, lax.rem(p1 + n1 - s, n1))]

        def forward_all(s, go):
            @pl.when(x == owner_x)
            def _():
                for event, block in blocks_of(s):
                    forward(event, block, go)

        forward_all(0, "start")
        started += gather_ring(
            n1, p1, dev1, 0, b1, g1s, g1r, lambda s: forward_all(s, "start")
        )
        for cp in started:
            cp.wait_send()
        for s in range(n1 // 2 + 1):
            forward_all(s, "wait")

        @pl.when(x == owner_x)
        def _():
            left[...] = full[:, pl.ds(lcol, 128)]

        @pl.when(x != owner_x)
        def _():
            for s in range(n1 // 2 + 1):
                for event, block in blocks_of(s):
                    at = pl.ds(pl.multiple_of(block * b1, 8), b1)
                    remote(left.at[at], left.at[at], fws.at[event, 0], fwr.at[event], c, x).wait_recv()

    along_y = (NY, y, lambda q: cal_of(z, q))
    along_z = (NZ, z, lambda q: cal_of(q, y))

    @pl.when(core == 0)
    def _():
        plane(along_y, along_z)

    @pl.when(core == 1)
    def _():
        plane(along_z, along_y)

    lt = left[...].T
    lhi, llo = split(lt)
    lhs = jnp.concatenate([lhi, llo], axis=0)
    w = WIDTH // TILES
    for n in range(TILES):
        ghi, glo = split(full[:, n * w : (n + 1) * w])
        both = jnp.dot(lhs, ghi, preferred_element_type=F32)
        low = jnp.dot(lhi, glo, preferred_element_type=F32)
        term = both[:128] + (both[128:] + low)
        mpart[:, n * w : (n + 1) * w] = term
    ours = pl.ds(pl.multiple_of(core * 64, 64), 64)
    other = pl.ds(pl.multiple_of((1 - core) * 64, 64), 64)
    m = remote(mpart.at[other], mrx, m_send, m_recv, sib, x)
    m.start()
    m.wait()
    out_ref[...] = (mpart[ours, :] + mrx[...]) * F32(1.0 / 131072)


def per_device(features, coef, log_exposure, claims, cluster_id, period, period_effect):
    vmem = pl.BlockSpec(memory_space=pltpu.VMEM)
    dma = pltpu.SemaphoreType.DMA
    scratch = [
        pltpu.VMEM((ROWS, WIDTH), BF16),
        pltpu.VMEM((16, WIDTH), BF16),
        pltpu.VMEM((NX, 16, 128), F32),
        pltpu.VMEM((16, 128), F32),
        pltpu.VMEM((HALF, ROWS), BF16),
        pltpu.VMEM((HALF, WIDTH), F32),
        pltpu.VMEM((HALF, WIDTH), F32),
        pltpu.VMEM((HALF, WIDTH), F32),
        pltpu.VMEM((2, 224, WIDTH), F32),
        pltpu.VMEM((2, 56, WIDTH), F32),
        pltpu.VMEM((HALF, WIDTH), F32),
        pltpu.VMEM((HALF, 128), F32),
        pltpu.VMEM((128, WIDTH), F32),
        pltpu.VMEM((64, WIDTH), F32),
        dma((FCH,)),
        dma((NX - 1,)),
        dma((NX - 1,)),
        dma((TILES,)),
        dma((TILES,)),
    ]
    scratch += [dma((2, 4)) for _ in range(8)]
    scratch += [dma((8, NX - 1)), dma((8,)), dma, dma]
    return pl.pallas_call(
        kernel,
        out_shape=jax.ShapeDtypeStruct((64, WIDTH), F32),
        in_specs=[pl.BlockSpec(memory_space=pl.ANY)] + [vmem] * 6,
        out_specs=vmem,
        scratch_shapes=scratch,
        compiler_params=pltpu.CompilerParams(
            collective_id=0, has_side_effects=True, vmem_limit_bytes=56 << 20
        ),
    )(
        features,
        coef.reshape(8, 128),
        log_exposure.reshape(16, 128),
        claims.reshape(16, 128),
        cluster_id.reshape(16, 128),
        period.reshape(16, 128),
        period_effect.reshape(1, 128),
    )


def solution(mesh):
    placed = (P("cal", "gr"), P("gr"), P("cal"), P("cal"), P("cal"), P("cal"), P())
    return jax.shard_map(
        per_device, mesh=mesh, in_specs=placed, out_specs=P("cal", "gr"), check_vma=False
    )
```

time: 415 us -> 92.4 us (0.22); the launches traced: 409 us -> 91.6 us
  waiting for transfers between devices: 335 us -> 0 us
  Pallas kernels: 0 us -> 90 us
  matrix products: 42.2 us -> 0 us
  blocking collectives: 14.8 us -> 0 us
  between operations: 13.5 us -> 0.01 us
    reduce_scatter x2 -> x0, waiting for transfers between devices: 335 us -> none  [the longest x1 193 us: per_device(): lax.psum_scatter(lax.dot_general(full_scores, owned, (((0,), (0,)), ((),...]
    pallas_call x0 -> x1, Pallas kernels: none -> 90 us  [per_device(): pl.pallas_call(kernel, out_shape=jax.ShapeDtypeStruct((64, WIDTH), F32),...]
    dot_general x6 -> x0, matrix products: 42.2 us -> none  [the longest x4 22.2 us: step(): lax.dot_general(picks, feat_blk, (((0,), (0,)), ((), ())), preferred_elem...]
    all_gather x1 -> x0, blocking collectives: 8.36 us -> none  [per_device(): full_scores = lax.all_gather(owned, 'gr', axis=1, tiled=True)]
    psum x1 -> x0, blocking collectives: 6.4 us -> none  [per_device(): linear = lax.psum(local_lin, 'gr')]
  transfers between devices with their start and end apart: 2 -> 0, of which waited for: 2 -> 0; matrix products, arithmetic and copies ran while one was open for 0% -> 0% of each run, Pallas kernels for 0% -> 0%
where the time goes in v1:
time: 92.4 us; the launch traced here: 91.6 us
  Pallas kernels  90 us (97%)
  local copies, waits for them, and re-layouts  1.67 us (2%)
    pallas_call x1, Pallas kernels, per_device(): pl.pallas_call(kernel, out_shape=jax.ShapeDtypeStruct((64, WIDTH), F32),...  90 us

profile of v1, /device:TPU:37, one launch (start us, length us, event | category | flops | bytes accessed | tf_op | source)
XLA Modules:
  0.0 91.6 jit_solution(3215221514303312710)
XLA Ops:
  0.0 90.0 %shard_map.73 = f32[64,1024]{1,0:T(8,128)} custom-call(bf16[2048,1024]{1,0:T(8,128)(2,1)} %feat_hbm.1, bf16[8,128]{1,0:T(8,128)(2,1)} %bitcast.10, f32[16,128]{1,0:T(8,128)} %bitcast.6, f32[16,128]{1,0:T(8,128)} %bitcast.7, s32[16,128]{1,0:T(8,128)} %bitcast.8, s32[16,128]{1,0:T(8,128)} %bitcast.9, f32[1,128]{1,0:T(1,128)} %bitcast.11), custom_call_target="tpu_custom_call" | custom-call | tf_op jit(solution)/shard_map/pallas_call | solution.py:311
  90.0 1.7 %copy.9 = f32[64,1024]{1,0:T(8,128)} copy(f32[64,1024]{1,0:T(8,128)} %shard_map.73) | data formatting | bytes 524288

commit v2 on v1

v2 whole, which is shorter than its diff:
```python
import jax
import jax.numpy as jnp
from jax import lax
from jax.experimental import pallas as pl
from jax.experimental.pallas import tpu as pltpu
from jax.sharding import PartitionSpec as P

NZ, NY, NX = 8, 4, 4
ROWS = 2048
WIDTH = 1024
HALF = 512
FCH = 4
CHUNKS = 2
CW = WIDTH // CHUNKS
RING4 = [[(2, 1, 0), (-2, -1, 1)], [(1, 0, None), (-1, 0, None)]]
DIRECT4 = [[(2, 0, None), (1, 0, None), (-1, 0, None)]]
RING8 = [[(4, 3, 0), (-4, -3, 1)]] + [[(k, k - 1, None), (-k, 1 - k, None)] for k in (3, 2, 1)]
THREE8 = [
    [(4, 2, 0), (-4, -2, 1), (3, 2, None), (-3, -2, None)],
    [(2, 1, None), (-2, -1, None)],
    [(1, 0, None), (-1, 0, None)],
]
TWO8 = [
    [(4, 2, 0), (-4, -2, 1), (3, 2, None), (-3, -2, None), (1, 0, None), (-1, 0, None)],
    [(2, 0, None), (-2, 0, None)],
]
DIRECT8 = [[(4, 0, None)] + [(s * k, 0, None) for k in (3, 2, 1) for s in (1, -1)]]
BIG = {"y": RING4, "z": RING8}
SMALL = {"y": DIRECT4, "z": TWO8}
FIRST = ("yyyy", "zzzz")
EDGES = 8
F32 = jnp.float32
SKEW = 0
BF16 = jnp.bfloat16


def remote(src, dst, send, recv, cal, gr):
    return pltpu.make_async_remote_copy(
        src_ref=src,
        dst_ref=dst,
        send_sem=send,
        recv_sem=recv,
        device_id=(cal, gr),
        device_id_type=pl.DeviceIdType.MESH,
    )


def split(v):
    hi = v.astype(BF16)
    lo = (v - hi.astype(F32)).astype(BF16)
    return hi, lo


def kernel(
    feat_hbm, coef_ref, logexp_ref, claims_ref, ids_ref, period_ref, effect_ref, out_ref,
    feat, cbuf, lin, res, picks, theirs, mine, core_rx, rx1, rx2, full, left, mpart, mrx,
    feat_sem, lin_send, lin_recv, core_send, core_recv,
    r1s, r1r, r2s, r2r, g1s, g1r, g2s, g2r, fws, fwr, m_send, m_recv,
):
    c = lax.axis_index("cal")
    x = lax.axis_index("gr")
    core = lax.rem(c, 2)
    y = lax.rem(lax.div(c, 2), NY)
    z = lax.div(c, 2 * NY)
    sib = c + 1 - 2 * core

    def cal_of(zz, yy):
        return (zz * NY + yy) * 2 + core

    fetches = []
    fr = ROWS // FCH
    for k in range(FCH):
        f = pltpu.make_async_copy(
            feat_hbm.at[pl.ds(k * fr, fr)], feat.at[pl.ds(k * fr, fr)], feat_sem.at[k]
        )
        f.start()
        fetches.append(f)

    barrier = pltpu.get_barrier_semaphore()
    peers = [(sib, x)]
    peers += [(c, lax.rem(x + k, NX)) for k in range(1, NX)]
    peers += [(cal_of(z, lax.rem(y + k, NY)), x) for k in range(1, NY)]
    peers += [(cal_of(lax.rem(z + k, NZ), y), x) for k in range(1, NZ)]
    for cal, gr in peers:
        pl.semaphore_signal(
            barrier, inc=1, device_id=(cal, gr), device_id_type=pl.DeviceIdType.MESH
        )

    cf = coef_ref[...].astype(F32)
    for j in range(WIDTH // 128):
        cbuf[:, j * 128 : (j + 1) * 128] = jnp.broadcast_to(cf[j : j + 1, :], (16, 128)).astype(BF16)
    for k in range(FCH):
        fetches[k].wait()
        part = lax.dot_general(
            cbuf[...], feat[k * fr : (k + 1) * fr, :], (((1,), (1,)), ((), ())),
            preferred_element_type=F32,
        )
        for j in range(fr // 128):
            lin[x, k * (fr // 128) + j, :] = part[0, j * 128 : (j + 1) * 128]
    pl.semaphore_wait(barrier, len(peers))

    for k in range(1, NX):
        to = lax.rem(x + k, NX)
        remote(lin.at[x], lin.at[x], lin_send.at[k - 1], lin_recv.at[k - 1], c, to).start()
    eff = effect_ref[...]
    where = lax.broadcasted_iota(jnp.int32, (1, 128), 1)
    d = c * 2
    e0 = jnp.sum(jnp.where(where == d, eff, 0.0), axis=1, keepdims=True)
    e1 = jnp.sum(jnp.where(where == d + 1, eff, 0.0), axis=1, keepdims=True)
    per = period_ref[...]
    shift = jnp.where(per == d, e0, jnp.where(per == d + 1, e1, 0.0))
    for k in range(1, NX):
        src = lax.rem(x + NX - k, NX)
        remote(lin.at[src], lin.at[src], lin_send.at[k - 1], lin_recv.at[k - 1], c, x).wait()
    linear = lin[0] + lin[1] + lin[2] + lin[3]
    value = claims_ref[...] - jnp.exp(linear + logexp_ref[...] + shift)
    res[...] = value.astype(BF16).astype(F32)

    def build(half, base):
        def column(j, carry):
            row = lax.broadcasted_iota(jnp.int32, (HALF, 128), 0) + base
            hit = row == ids_ref[pl.ds(j, 1), :]
            col = pl.ds(pl.multiple_of(j * 128, 128), 128)
            picks[half, :, col] = jnp.where(hit, res[pl.ds(j, 1), :], 0.0).astype(BF16)
            return carry

        lax.fori_loop(0, ROWS // 128, column, 0)

    def product(n, half, dst):
        dst[n] = jnp.dot(picks[half], feat[:, n * CW : (n + 1) * CW], preferred_element_type=F32)

    def push(n):
        return remote(theirs.at[n], core_rx.at[n], core_send.at[n], core_recv.at[n], sib, x)

    def fold(n):
        push(n).wait_recv()
        mine[n] += core_rx[n]

    owner_x = lax.div(z, 2)
    place = lax.rem(z, 2) * NY + y
    lchunk = lax.div(place, CW // 128)
    lcol = pl.multiple_of(lax.rem(place, CW // 128) * 128, 128)
    axes = {
        "y": (NY, y, lambda q: cal_of(z, q)),
        "z": (NZ, z, lambda q: cal_of(q, y)),
    }

    def rows_of(base, n, place, rows, half):
        start = base + lax.rem(place + 2 * n, n) * rows
        if half is not None:
            rows = rows // 2
            start = start + half * rows
        return pl.ds(pl.multiple_of(start, 8), rows)

    def slots_of(tree, rows):
        at, slots = 0, []
        for rnd in tree:
            for a, b, half in rnd:
                size = rows if half is None else rows // 2
                slots.append((a, b, half, pl.ds(at, size)))
                at += size
        return slots

    def plan(k, first):
        second = "z" if first == "y" else "y"
        n1, p1, dev1 = axes[first]
        n2, p2, dev2 = axes[second]
        b1 = HALF // n1
        b2 = b1 // n2
        base2 = p1 * b1
        steps, ends = [], []

        def sum_steps(tree, n, p, dev, base, rows, rx, ss, rs):
            slots = slots_of(tree, rows)

            def edge(i):
                a, b, half, slot = slots[i]
                blk = rows_of(base, n, p - a, rows, half)
                to = dev(lax.rem(p - a + b + 2 * n, n))
                return remote(mine.at[k, blk], rx.at[k, slot], ss.at[k, i], rs.at[k, i], to, x)

            def take(place):
                for i, (_, b, half, slot) in enumerate(slots):
                    if b == place:
                        edge(i).wait_recv()
                        mine[k, rows_of(base, n, p - b, rows, half), :] += rx[k, slot, :]

            def send(lo, hi):
                done = set()
                for i in range(lo, hi):
                    a = slots[i][0]
                    if a not in done:
                        done.add(a)
                        take(a)
                    edge(i).start()

            at = 0
            for rnd in tree:
                steps.append(lambda lo=at, hi=at + len(rnd): send(lo, hi))
                at += len(rnd)
            ends.extend(lambda i=i: edge(i).wait_send() for i in range(at))
            return lambda: take(0)

        def gather_steps(tree, n, p, dev, base, rows, ss, rs, got):
            slots = slots_of(tree, rows)

            def edge(i, receive=False):
                a, b, half, _ = slots[i]
                at = a if receive else b
                blk = rows_of(base, n, p - at, rows, half)
                to = dev(lax.rem(p - b + a + 2 * n, n))
                return remote(full.at[k, blk], full.at[k, blk], ss.at[k, i], rs.at[k, i], to, x)

            def take(place):
                for i, (a, _, _, _) in enumerate(slots):
                    if a == place:
                        edge(i, True).wait_recv()
                        got(place)

            def send(lo, hi):
                done = set()
                for i in range(lo, hi):
                    b = slots[i][1]
                    if b not in done:
                        done.add(b)
                        if b != 0:
                            take(b)
                    edge(i).start()

            at = len(slots)
            for rnd in reversed(tree):
                steps.append(lambda lo=at - len(rnd), hi=at: send(lo, hi))
                at -= len(rnd)
            ends.extend(lambda i=i: edge(i).wait_send() for i in range(len(slots)))

            def rest():
                inner = {b for _, b, _, _ in slots}
                seen = set()
                for a, _, _, _ in slots:
                    if a not in inner and a not in seen:
                        seen.add(a)
                        take(a)

            return rest

        def chain(done, more):
            def both():
                done()
                more()

            return both

        end1 = sum_steps(BIG[first], n1, p1, dev1, 0, b1, rx1, r1s, r1r)
        mark = len(steps)
        end2 = sum_steps(SMALL[second], n2, p2, dev2, base2, b2, rx2, r2s, r2r)
        steps[mark] = chain(end1, steps[mark])
        mark = len(steps)

        def own():
            end2()
            at = rows_of(base2, n2, p2, b2, None)
            full[k, at, :] = mine[k, at, :]

        end3 = gather_steps(SMALL[second], n2, p2, dev2, base2, b2, g2s, g2r, lambda place: None)
        steps[mark] = chain(own, steps[mark])
        mark = len(steps)

        sends = {}

        def forward(event, place, half):
            at = rows_of(0, n1, p1 - place, b1, half)
            src = full.at[k, at, pl.ds(lcol, 128)]
            return [
                remote(src, left.at[at], fws.at[event, q - 1], fwr.at[event], c, lax.rem(x + q, NX))
                for q in range(1, NX)
            ]

        mine_to_send = jnp.logical_and(x == owner_x, lchunk == k)
        mine_to_get = jnp.logical_and(x != owner_x, lchunk == k)

        def out(place):
            sends[place] = len(sends)

            @pl.when(mine_to_send)
            def _():
                for cp in forward(sends[place], place, None):
                    cp.start()

        slots1 = slots_of(BIG[first], b1)
        counts = {}
        for a, _, _, _ in slots1:
            key = a % n1
            counts[key] = counts.get(key, 0) + 1
        left_over = dict(counts)

        def got(place):
            key = place % n1
            left_over[key] -= 1
            if left_over[key] == 0:
                out(key)

        def begin():
            end3()
            out(0)

        end4 = gather_steps(BIG[first], n1, p1, dev1, 0, b1, g1s, g1r, got)
        steps[mark] = chain(begin, steps[mark])
        steps.append(end4)

        def finish():
            for e in ends:
                e()

            @pl.when(mine_to_send)
            def _():
                for place, event in sends.items():
                    for cp in forward(event, place, None):
                        cp.wait_send()
                left[...] = full[k, :, pl.ds(lcol, 128)]

            @pl.when(mine_to_get)
            def _():
                for place, event in sends.items():
                    at = rows_of(0, n1, p1 - place, b1, None)
                    remote(left.at[at], left.at[at], fws.at[event, 0], fwr.at[event], c, x).wait_recv()

        return steps, finish

    plans = [[plan(k, FIRST[h][k]) for k in range(CHUNKS)] for h in (0, 1)]

    def comm(k, s):
        for h in (0, 1):
            steps = plans[h][k][0]
            if s < len(steps):
                pl.when(core == h)(steps[s])

    build(0, (1 - core) * HALF)
    for k in range(CHUNKS):
        product(k, 0, theirs)
        push(k).start()
        if k == 0:
            build(1, core * HALF)
        product(k, 1, mine)
        if k > 0:
            fold(k - 1)
            comm(k - 1, 0)
        if k > 2:
            comm(k - 3, 1)
    fold(CHUNKS - 1)
    comm(CHUNKS - 1, 0)
    total = max(len(p[0]) for h in (0, 1) for p in plans[h])
    for s in range(1, total + SKEW * CHUNKS):
        for k in range(CHUNKS):
            at = s - SKEW * k
            if at >= (2 if k + 3 < CHUNKS else 1) and at < total:
                comm(k, at)
    for k in range(CHUNKS):
        push(k).wait_send()
        for h in (0, 1):
            pl.when(core == h)(plans[h][k][1])

    lt = left[...].T
    lhi, llo = split(lt)
    lhs = jnp.concatenate([lhi, llo], axis=0)
    for n in range(CHUNKS):
        ghi, glo = split(full[n])
        both = jnp.dot(lhs, ghi, preferred_element_type=F32)
        low = jnp.dot(lhi, glo, preferred_element_type=F32)
        mpart[:, n * CW : (n + 1) * CW] = both[:128] + (both[128:] + low)
    ours = pl.ds(pl.multiple_of(core * 64, 64), 64)
    other = pl.ds(pl.multiple_of((1 - core) * 64, 64), 64)
    m = remote(mpart.at[other], mrx, m_send, m_recv, sib, x)
    m.start()
    m.wait()
    out_ref[...] = (mpart[ours, :] + mrx[...]) * F32(1.0 / 131072)


def per_device(features, coef, log_exposure, claims, cluster_id, period, period_effect):
    vmem = pl.BlockSpec(memory_space=pltpu.VMEM)
    dma = pltpu.SemaphoreType.DMA
    chunked = pltpu.VMEM((CHUNKS, HALF, CW), F32)
    scratch = [
        pltpu.VMEM((ROWS, WIDTH), BF16),
        pltpu.VMEM((16, WIDTH), BF16),
        pltpu.VMEM((NX, 16, 128), F32),
        pltpu.VMEM((16, 128), F32),
        pltpu.VMEM((2, HALF, ROWS), BF16),
        chunked,
        chunked,
        chunked,
        pltpu.VMEM((CHUNKS, 448, CW), F32),
        pltpu.VMEM((CHUNKS, 112, CW), F32),
        chunked,
        pltpu.VMEM((HALF, 128), F32),
        pltpu.VMEM((128, WIDTH), F32),
        pltpu.VMEM((64, WIDTH), F32),
        dma((FCH,)),
        dma((NX - 1,)),
        dma((NX - 1,)),
        dma((CHUNKS,)),
        dma((CHUNKS,)),
    ]
    scratch += [dma((CHUNKS, EDGES)) for _ in range(8)]
    scratch += [dma((8, NX - 1)), dma((8,)), dma, dma]
    return pl.pallas_call(
        kernel,
        out_shape=jax.ShapeDtypeStruct((64, WIDTH), F32),
        in_specs=[pl.BlockSpec(memory_space=pl.ANY)] + [vmem] * 6,
        out_specs=vmem,
        scratch_shapes=scratch,
        compiler_params=pltpu.CompilerParams(
            collective_id=0, has_side_effects=True, vmem_limit_bytes=56 << 20
        ),
    )(
        features,
        coef.reshape(8, 128),
        log_exposure.reshape(16, 128),
        claims.reshape(16, 128),
        cluster_id.reshape(16, 128),
        period.reshape(16, 128),
        period_effect.reshape(1, 128),
    )


def solution(mesh):
    placed = (P("cal", "gr"), P("gr"), P("cal"), P("cal"), P("cal"), P("cal"), P())
    return jax.shard_map(
        per_device, mesh=mesh, in_specs=placed, out_specs=P("cal", "gr"), check_vma=False
    )
```

time: 92.4 us -> 68.3 us (0.74)
  Pallas kernels: 90 us -> 66.5 us
    pallas_call x1, Pallas kernels: 90 us -> 66.5 us  [per_device(): pl.pallas_call(kernel, out_shape=jax.ShapeDtypeStruct((64, WIDTH), F32),...]
where the time goes in v2:
time: 68.3 us; the launch traced here: 68.2 us
  Pallas kernels  66.5 us (97%)
  local copies, waits for them, and re-layouts  1.67 us (2%)
    pallas_call x1, Pallas kernels, per_device(): pl.pallas_call(kernel, out_shape=jax.ShapeDtypeStruct((64, WIDTH), F32),...  66.5 us
    unnamed x1, local copies, waits for them, and re-layouts  1.67 us

profile of v2, /device:TPU:37, one launch (start us, length us, event | category | flops | bytes accessed | tf_op | source)
XLA Modules:
  0.0 68.2 jit_solution(8835588033617826561)
XLA Ops:
  0.0 66.5 %shard_map.73 = f32[64,1024]{1,0:T(8,128)} custom-call(bf16[2048,1024]{1,0:T(8,128)(2,1)} %feat_hbm.1, bf16[8,128]{1,0:T(8,128)(2,1)} %bitcast.10, f32[16,128]{1,0:T(8,128)} %bitcast.6, f32[16,128]{1,0:T(8,128)} %bitcast.7, s32[16,128]{1,0:T(8,128)} %bitcast.8, s32[16,128]{1,0:T(8,128)} %bitcast.9, f32[1,128]{1,0:T(1,128)} %bitcast.11), custom_call_target="tpu_custom_call" | custom-call | tf_op jit(solution)/shard_map/pallas_call | solution.py:405
  66.5 1.7 %copy.9 = f32[64,1024]{1,0:T(8,128)} copy(f32[64,1024]{1,0:T(8,128)} %shard_map.73) | data formatting | bytes 524288

commit v3 on v2

--- a/solution.py
+++ b/solution.py
@@ -10,7 +10,7 @@
 WIDTH = 1024
 HALF = 512
 FCH = 4
-CHUNKS = 2
+CHUNKS = 4
 CW = WIDTH // CHUNKS
 RING4 = [[(2, 1, 0), (-2, -1, 1)], [(1, 0, None), (-1, 0, None)]]
 DIRECT4 = [[(2, 0, None), (1, 0, None), (-1, 0, None)]]
@@ -27,11 +27,18 @@
 DIRECT8 = [[(4, 0, None)] + [(s * k, 0, None) for k in (3, 2, 1) for s in (1, -1)]]
 BIG = {"y": RING4, "z": RING8}
 SMALL = {"y": DIRECT4, "z": TWO8}
-FIRST = ("yyyy", "zzzz")
+FIRST = "yz"
+UNIT = 128
 EDGES = 8
 F32 = jnp.float32
-SKEW = 0
+UNROLL = 4
+AHEAD = 1
+ZPEERS = (1, 2, NZ - 2, NZ - 1)
 BF16 = jnp.bfloat16
+
+
+def order(n):
+    return [n // 2] + [w * d % n for d in range(n // 2 - 1, 0, -1) for w in (1, -1)] + [0]
 
 
 def remote(src, dst, send, recv, cal, gr):
@@ -55,7 +62,7 @@
     feat_hbm, coef_ref, logexp_ref, claims_ref, ids_ref, period_ref, effect_ref, out_ref,
     feat, cbuf, lin, res, picks, theirs, mine, core_rx, rx1, rx2, full, left, mpart, mrx,
     feat_sem, lin_send, lin_recv, core_send, core_recv,
-    r1s, r1r, r2s, r2r, g1s, g1r, g2s, g2r, fws, fwr, m_send, m_recv,
+    sum_send, gat_send, r1r, r2r, g1r, g2r, fws, fwr, m_send, m_recv,
 ):
     c = lax.axis_index("cal")
     x = lax.axis_index("gr")
@@ -80,7 +87,7 @@
     peers = [(sib, x)]
     peers += [(c, lax.rem(x + k, NX)) for k in range(1, NX)]
     peers += [(cal_of(z, lax.rem(y + k, NY)), x) for k in range(1, NY)]
-    peers += [(cal_of(lax.rem(z + k, NZ), y), x) for k in range(1, NZ)]
+    peers += [(cal_of(lax.rem(z + k, NZ), y), x) for k in ZPEERS]
     for cal, gr in peers:
         pl.semaphore_signal(
             barrier, inc=1, device_id=(cal, gr), device_id_type=pl.DeviceIdType.MESH
@@ -116,41 +123,72 @@
     value = claims_ref[...] - jnp.exp(linear + logexp_ref[...] + shift)
     res[...] = value.astype(BF16).astype(F32)
 
-    def build(half, base):
+    ring_y = [lax.rem(y + k, NY) for k in range(NY)]
+    ring_z = [lax.rem(z + k, NZ) for k in range(NZ)]
+    axes = {
+        "y": (NY, ring_y, [cal_of(z, q) for q in ring_y]),
+        "z": (NZ, ring_z, [cal_of(q, y) for q in ring_z]),
+    }
+
+    def firsts(h):
+        (n1, p1, _), (n2, p2, _) = axes[FIRST[h]], axes["z" if FIRST[h] == "y" else "y"]
+        b1 = HALF // n1
+        b2 = b1 // n2
+        return [h * HALF + p1[d1] * b1 + p2[d2] * b2 for d1 in order(n1) for d2 in order(n2)]
+
+    groups = [
+        [jnp.where(core == half, v1, v0) for v0, v1 in zip(firsts(0), firsts(1))] for half in (0, 1)
+    ]
+    few = HALF // len(groups[0])
+
+    def build(half, unit):
         def column(j, carry):
-            row = lax.broadcasted_iota(jnp.int32, (HALF, 128), 0) + base
-            hit = row == ids_ref[pl.ds(j, 1), :]
+            row = lax.broadcasted_iota(jnp.int32, (few, 128), 0)
+            ids = ids_ref[pl.ds(j, 1), :]
+            val = jnp.broadcast_to(res[pl.ds(j, 1), :], (few, 128))
             col = pl.ds(pl.multiple_of(j * 128, 128), 128)
-            picks[half, :, col] = jnp.where(hit, res[pl.ds(j, 1), :], 0.0).astype(BF16)
+            for g in range(unit * UNIT // few, (unit + 1) * UNIT // few):
+                hit = row == ids - groups[half][g]
+                picks[half, g * few : (g + 1) * few, col] = jnp.where(hit, val, 0.0).astype(BF16)
             return carry
 
         lax.fori_loop(0, ROWS // 128, column, 0)
 
-    def product(n, half, dst):
-        dst[n] = jnp.dot(picks[half], feat[:, n * CW : (n + 1) * CW], preferred_element_type=F32)
-
-    def push(n):
-        return remote(theirs.at[n], core_rx.at[n], core_send.at[n], core_recv.at[n], sib, x)
-
-    def fold(n):
-        push(n).wait_recv()
-        mine[n] += core_rx[n]
+    def product(half, unit, dst):
+        build(half, unit)
+        here = slice(unit * UNIT, (unit + 1) * UNIT)
+        for n in range(CHUNKS):
+            dst[n, here, :] = jnp.dot(
+                picks[half, here, :], feat[:, n * CW : (n + 1) * CW], preferred_element_type=F32
+            )
+
+    def push(u):
+        here = pl.ds(u * UNIT, UNIT)
+        return remote(
+            theirs.at[:, here], core_rx.at[:, here], core_send.at[u], core_recv.at[u], sib, x
+        )
+
+    def make(u):
+        product(0, u, theirs)
+        push(u).start()
+        product(1, u, mine)
+
+    def fold(u):
+        push(u).wait_recv()
+        here = slice(u * UNIT, (u + 1) * UNIT)
+        for n in range(CHUNKS):
+            mine[n, here, :] += core_rx[n, here, :]
 
     owner_x = lax.div(z, 2)
     place = lax.rem(z, 2) * NY + y
     lchunk = lax.div(place, CW // 128)
     lcol = pl.multiple_of(lax.rem(place, CW // 128) * 128, 128)
-    axes = {
-        "y": (NY, y, lambda q: cal_of(z, q)),
-        "z": (NZ, z, lambda q: cal_of(q, y)),
-    }
-
     def rows_of(base, n, place, rows, half):
-        start = base + lax.rem(place + 2 * n, n) * rows
+        start = base + order(n).index(place % n) * rows
         if half is not None:
             rows = rows // 2
             start = start + half * rows
-        return pl.ds(pl.multiple_of(start, 8), rows)
+        return pl.ds(start, rows)
 
     def slots_of(tree, rows):
         at, slots = 0, []
@@ -161,29 +199,37 @@
                 at += size
         return slots
 
+    def add(k, start, rx, slot):
+        def tile(j, carry):
+            here = pl.ds(pl.multiple_of(start + j * 8, 8), 8)
+            mine[k, here, :] += rx[k, pl.ds(pl.multiple_of(slot.start + j * 8, 8), 8), :]
+            return carry
+
+        lax.fori_loop(0, slot.size // 8, tile, 0, unroll=min(UNROLL, slot.size // 8))
+
     def plan(k, first):
         second = "z" if first == "y" else "y"
         n1, p1, dev1 = axes[first]
         n2, p2, dev2 = axes[second]
         b1 = HALF // n1
         b2 = b1 // n2
-        base2 = p1 * b1
-        steps, ends = [], []
+        base2 = HALF - b1
+        needs = []
+        steps = []
 
         def sum_steps(tree, n, p, dev, base, rows, rx, ss, rs):
             slots = slots_of(tree, rows)
 
             def edge(i):
                 a, b, half, slot = slots[i]
-                blk = rows_of(base, n, p - a, rows, half)
-                to = dev(lax.rem(p - a + b + 2 * n, n))
-                return remote(mine.at[k, blk], rx.at[k, slot], ss.at[k, i], rs.at[k, i], to, x)
+                blk = rows_of(base, n, -a, rows, half)
+                return remote(mine.at[k, blk], rx.at[k, slot], ss.at[k], rs.at[k, i], dev[(b - a) % n], x)
 
             def take(place):
                 for i, (_, b, half, slot) in enumerate(slots):
                     if b == place:
                         edge(i).wait_recv()
-                        mine[k, rows_of(base, n, p - b, rows, half), :] += rx[k, slot, :]
+                        add(k, rows_of(base, n, -b, rows, half).start, rx, slot)
 
             def send(lo, hi):
                 done = set()
@@ -196,25 +242,25 @@
 
             at = 0
             for rnd in tree:
+                blks = [rows_of(base, n, -a, rows, None) for a, _, _ in rnd]
+                needs.append(max(blk.start + blk.size for blk in blks))
                 steps.append(lambda lo=at, hi=at + len(rnd): send(lo, hi))
                 at += len(rnd)
-            ends.extend(lambda i=i: edge(i).wait_send() for i in range(at))
             return lambda: take(0)
 
         def gather_steps(tree, n, p, dev, base, rows, ss, rs, got):
             slots = slots_of(tree, rows)
 
-            def edge(i, receive=False):
+            def edge(i):
                 a, b, half, _ = slots[i]
-                at = a if receive else b
-                blk = rows_of(base, n, p - at, rows, half)
-                to = dev(lax.rem(p - b + a + 2 * n, n))
-                return remote(full.at[k, blk], full.at[k, blk], ss.at[k, i], rs.at[k, i], to, x)
+                src = full.at[k, rows_of(base, n, -b, rows, half)]
+                dst = full.at[k, rows_of(base, n, -a, rows, half)]
+                return remote(src, dst, ss.at[k], rs.at[k, i], dev[(a - b) % n], x)
 
             def take(place):
                 for i, (a, _, _, _) in enumerate(slots):
                     if a == place:
-                        edge(i, True).wait_recv()
+                        edge(i).wait_recv()
                         got(place)
 
             def send(lo, hi):
@@ -231,7 +277,6 @@
             for rnd in reversed(tree):
                 steps.append(lambda lo=at - len(rnd), hi=at: send(lo, hi))
                 at -= len(rnd)
-            ends.extend(lambda i=i: edge(i).wait_send() for i in range(len(slots)))
 
             def rest():
                 inner = {b for _, b, _, _ in slots}
@@ -250,25 +295,25 @@
 
             return both
 
-        end1 = sum_steps(BIG[first], n1, p1, dev1, 0, b1, rx1, r1s, r1r)
+        end1 = sum_steps(BIG[first], n1, p1, dev1, 0, b1, rx1, sum_send, r1r)
         mark = len(steps)
-        end2 = sum_steps(SMALL[second], n2, p2, dev2, base2, b2, rx2, r2s, r2r)
+        end2 = sum_steps(SMALL[second], n2, p2, dev2, base2, b2, rx2, sum_send, r2r)
         steps[mark] = chain(end1, steps[mark])
         mark = len(steps)
 
         def own():
             end2()
-            at = rows_of(base2, n2, p2, b2, None)
+            at = rows_of(base2, n2, 0, b2, None)
             full[k, at, :] = mine[k, at, :]
 
-        end3 = gather_steps(SMALL[second], n2, p2, dev2, base2, b2, g2s, g2r, lambda place: None)
+        end3 = gather_steps(SMALL[second], n2, p2, dev2, base2, b2, gat_send, g2r, lambda place: None)
         steps[mark] = chain(own, steps[mark])
         mark = len(steps)
 
         sends = {}
 
         def forward(event, place, half):
-            at = rows_of(0, n1, p1 - place, b1, half)
+            at = rows_of(0, n1, -place, b1, half)
             src = full.at[k, at, pl.ds(lcol, 128)]
             return [
                 remote(src, left.at[at], fws.at[event, q - 1], fwr.at[event], c, lax.rem(x + q, NX))
@@ -303,13 +348,14 @@
             end3()
             out(0)
 
-        end4 = gather_steps(BIG[first], n1, p1, dev1, 0, b1, g1s, g1r, got)
+        end4 = gather_steps(BIG[first], n1, p1, dev1, 0, b1, gat_send, g1r, got)
         steps[mark] = chain(begin, steps[mark])
         steps.append(end4)
 
         def finish():
-            for e in ends:
-                e()
+            sent = pl.ds(0, HALF - b2)
+            remote(mine.at[k, sent], mine.at[k, sent], sum_send.at[k], r1r.at[k, 0], c, x).wait_send()
+            remote(full.at[k, sent], full.at[k, sent], gat_send.at[k], g1r.at[k, 0], c, x).wait_send()
 
             @pl.when(mine_to_send)
             def _():
@@ -321,12 +367,12 @@
             @pl.when(mine_to_get)
             def _():
                 for place, event in sends.items():
-                    at = rows_of(0, n1, p1 - place, b1, None)
+                    at = rows_of(0, n1, -place, b1, None)
                     remote(left.at[at], left.at[at], fws.at[event, 0], fwr.at[event], c, x).wait_recv()
 
-        return steps, finish
-
-    plans = [[plan(k, FIRST[h][k]) for k in range(CHUNKS)] for h in (0, 1)]
+        return steps, finish, needs
+
+    plans = [[plan(k, FIRST[h]) for k in range(CHUNKS)] for h in (0, 1)]
 
     def comm(k, s):
         for h in (0, 1):
@@ -334,28 +380,24 @@
             if s < len(steps):
                 pl.when(core == h)(steps[s])
 
-    build(0, (1 - core) * HALF)
+    units = HALF // UNIT
+    made = folded = 0
+    total = max(len(p[0]) for h in (0, 1) for p in plans[h])
+    for s in range(total):
+        upto = max(p[2][s] if s < len(p[2]) else HALF for h in (0, 1) for p in plans[h])
+        upto = -(-upto // UNIT)
+        ahead = min(units, max(upto + AHEAD, units if s else 0))
+        while made < ahead:
+            make(made)
+            made += 1
+        while folded < upto:
+            fold(folded)
+            folded += 1
+        for k in range(CHUNKS):
+            comm(k, s)
+    for u in range(units):
+        push(u).wait_send()
     for k in range(CHUNKS):
-        product(k, 0, theirs)
-        push(k).start()
-        if k == 0:
-            build(1, core * HALF)
-        product(k, 1, mine)
-        if k > 0:
-            fold(k - 1)
-            comm(k - 1, 0)
-        if k > 2:
-            comm(k - 3, 1)
-    fold(CHUNKS - 1)
-    comm(CHUNKS - 1, 0)
-    total = max(len(p[0]) for h in (0, 1) for p in plans[h])
-    for s in range(1, total + SKEW * CHUNKS):
-        for k in range(CHUNKS):
-            at = s - SKEW * k
-            if at >= (2 if k + 3 < CHUNKS else 1) and at < total:
-                comm(k, at)
-    for k in range(CHUNKS):
-        push(k).wait_send()
         for h in (0, 1):
             pl.when(core == h)(plans[h][k][1])
 
@@ -397,10 +439,11 @@
         dma((FCH,)),
         dma((NX - 1,)),
         dma((NX - 1,)),
-        dma((CHUNKS,)),
-        dma((CHUNKS,)),
+        dma((HALF // UNIT,)),
+        dma((HALF // UNIT,)),
     ]
-    scratch += [dma((CHUNKS, EDGES)) for _ in range(8)]
+    scratch += [dma((CHUNKS,)) for _ in range(2)]
+    scratch += [dma((CHUNKS, EDGES)) for _ in range(4)]
     scratch += [dma((8, NX - 1)), dma((8,)), dma, dma]
     return pl.pallas_call(
         kernel,

time: 68.3 us -> 63 us (0.922)
  Pallas kernels: 66.5 us -> 61.2 us
    pallas_call x1, Pallas kernels: 66.5 us -> 61.2 us  [per_device(): pl.pallas_call(kernel, out_shape=jax.ShapeDtypeStruct((64, WIDTH), F32),...]
where the time goes in v3:
time: 63 us; the launch traced here: 62.9 us
  Pallas kernels  61.2 us (97%)
  local copies, waits for them, and re-layouts  1.67 us (3%)
    pallas_call x1, Pallas kernels, per_device(): pl.pallas_call(kernel, out_shape=jax.ShapeDtypeStruct((64, WIDTH), F32),...  61.2 us
    unnamed x1, local copies, waits for them, and re-layouts  1.67 us

profile of v3, /device:TPU:37, one launch (start us, length us, event | category | flops | bytes accessed | tf_op | source)
XLA Modules:
  0.0 62.9 jit_solution(1424927370182347830)
XLA Ops:
  0.0 61.2 %shard_map.73 = f32[64,1024]{1,0:T(8,128)} custom-call(bf16[2048,1024]{1,0:T(8,128)(2,1)} %feat_hbm.1, bf16[8,128]{1,0:T(8,128)(2,1)} %bitcast.10, f32[16,128]{1,0:T(8,128)} %bitcast.6, f32[16,128]{1,0:T(8,128)} %bitcast.7, s32[16,128]{1,0:T(8,128)} %bitcast.8, s32[16,128]{1,0:T(8,128)} %bitcast.9, f32[1,128]{1,0:T(1,128)} %bitcast.11), custom_call_target="tpu_custom_call" | custom-call | tf_op jit(solution)/shard_map/pallas_call | solution.py:448
  61.2 1.7 %copy.9 = f32[64,1024]{1,0:T(8,128)} copy(f32[64,1024]{1,0:T(8,128)} %shard_map.73) | data formatting | bytes 524288

commit v4 on v3

--- a/solution.py
+++ b/solution.py
@@ -25,15 +25,19 @@
     [(2, 0, None), (-2, 0, None)],
 ]
 DIRECT8 = [[(4, 0, None)] + [(s * k, 0, None) for k in (3, 2, 1) for s in (1, -1)]]
+BIG_G = {"y": RING4, "z": RING8}
+SMALL_G = {"y": DIRECT4, "z": TWO8}
 BIG = {"y": RING4, "z": RING8}
 SMALL = {"y": DIRECT4, "z": TWO8}
 FIRST = "yz"
+LAST = "zy"
 UNIT = 128
 EDGES = 8
 F32 = jnp.float32
 UNROLL = 4
 AHEAD = 1
-ZPEERS = (1, 2, NZ - 2, NZ - 1)
+ZPEERS = (2, NZ - 2, 1, NZ - 1)
+FARX = (2, 1, 3)
 BF16 = jnp.bfloat16
 
 
@@ -59,8 +63,9 @@
 
 
 def kernel(
-    feat_hbm, coef_ref, logexp_ref, claims_ref, ids_ref, period_ref, effect_ref, out_ref,
-    feat, cbuf, lin, res, picks, theirs, mine, core_rx, rx1, rx2, full, left, mpart, mrx,
+    feat_hbm, coef_ref, logexp_hbm, claims_hbm, ids_hbm, period_hbm, effect_hbm, out_ref,
+    logexp_ref, claims_ref, ids_ref, period_ref, effect_ref, in_sem,
+    feat, cbuf, lin, res, picks, theirs, mine, core_rx, rx1, rx2, full, left, mpart, mrx, high, low,
     feat_sem, lin_send, lin_recv, core_send, core_recv,
     sum_send, gat_send, r1r, r2r, g1r, g2r, fws, fwr, m_send, m_recv,
 ):
@@ -74,6 +79,28 @@
     def cal_of(zz, yy):
         return (zz * NY + yy) * 2 + core
 
+    barrier = pltpu.get_barrier_semaphore()
+    peers = [(cal_of(lax.rem(z + k, NZ), y), x) for k in ZPEERS]
+    peers += [(cal_of(z, lax.rem(y + k, NY)), x) for k in (2, 1, NY - 1)]
+    peers += [(c, lax.rem(x + k, NX)) for k in FARX]
+    peers += [(sib, x)]
+    for cal, gr in peers:
+        pl.semaphore_signal(
+            barrier, inc=1, device_id=(cal, gr), device_id_type=pl.DeviceIdType.MESH
+        )
+
+    small = [
+        pltpu.make_async_copy(src, dst, in_sem.at[i])
+        for i, (src, dst) in enumerate(
+            [
+                (logexp_hbm, logexp_ref),
+                (claims_hbm, claims_ref),
+                (ids_hbm, ids_ref),
+                (period_hbm, period_ref),
+                (effect_hbm, effect_ref),
+            ]
+        )
+    ]
     fetches = []
     fr = ROWS // FCH
     for k in range(FCH):
@@ -82,16 +109,8 @@
         )
         f.start()
         fetches.append(f)
-
-    barrier = pltpu.get_barrier_semaphore()
-    peers = [(sib, x)]
-    peers += [(c, lax.rem(x + k, NX)) for k in range(1, NX)]
-    peers += [(cal_of(z, lax.rem(y + k, NY)), x) for k in range(1, NY)]
-    peers += [(cal_of(lax.rem(z + k, NZ), y), x) for k in ZPEERS]
-    for cal, gr in peers:
-        pl.semaphore_signal(
-            barrier, inc=1, device_id=(cal, gr), device_id_type=pl.DeviceIdType.MESH
-        )
+    for f in small:
+        f.start()
 
     cf = coef_ref[...].astype(F32)
     for j in range(WIDTH // 128):
@@ -104,9 +123,11 @@
         )
         for j in range(fr // 128):
             lin[x, k * (fr // 128) + j, :] = part[0, j * 128 : (j + 1) * 128]
+    for f in small:
+        f.wait()
     pl.semaphore_wait(barrier, len(peers))
 
-    for k in range(1, NX):
+    for k in FARX:
         to = lax.rem(x + k, NX)
         remote(lin.at[x], lin.at[x], lin_send.at[k - 1], lin_recv.at[k - 1], c, to).start()
     eff = effect_ref[...]
@@ -157,10 +178,11 @@
     def product(half, unit, dst):
         build(half, unit)
         here = slice(unit * UNIT, (unit + 1) * UNIT)
-        for n in range(CHUNKS):
-            dst[n, here, :] = jnp.dot(
-                picks[half, here, :], feat[:, n * CW : (n + 1) * CW], preferred_element_type=F32
-            )
+        wide = max(CW, 256)
+        for n in range(0, WIDTH, wide):
+            val = jnp.dot(picks[half, here, :], feat[:, n : n + wide], preferred_element_type=F32)
+            for q in range(wide // CW):
+                dst[n // CW + q, here, :] = val[:, q * CW : (q + 1) * CW]
 
     def push(u):
         here = pl.ds(u * UNIT, UNIT)
@@ -207,17 +229,17 @@
 
         lax.fori_loop(0, slot.size // 8, tile, 0, unroll=min(UNROLL, slot.size // 8))
 
-    def plan(k, first):
+    def plan(k, first, last):
         second = "z" if first == "y" else "y"
-        n1, p1, dev1 = axes[first]
-        n2, p2, dev2 = axes[second]
+        n1, _, dev1 = axes[first]
+        n2, _, dev2 = axes[second]
         b1 = HALF // n1
         b2 = b1 // n2
         base2 = HALF - b1
         needs = []
         steps = []
 
-        def sum_steps(tree, n, p, dev, base, rows, rx, ss, rs):
+        def sum_steps(tree, n, dev, base, rows, rx, ss, rs):
             slots = slots_of(tree, rows)
 
             def edge(i):
@@ -248,7 +270,7 @@
                 at += len(rnd)
             return lambda: take(0)
 
-        def gather_steps(tree, n, p, dev, base, rows, ss, rs, got):
+        def gather_steps(tree, n, dev, base, rows, ss, rs, got):
             slots = slots_of(tree, rows)
 
             def edge(i):
@@ -295,29 +317,35 @@
 
             return both
 
-        end1 = sum_steps(BIG[first], n1, p1, dev1, 0, b1, rx1, sum_send, r1r)
+        end1 = sum_steps(BIG[first], n1, dev1, 0, b1, rx1, sum_send, r1r)
         mark = len(steps)
-        end2 = sum_steps(SMALL[second], n2, p2, dev2, base2, b2, rx2, sum_send, r2r)
+        end2 = sum_steps(SMALL[second], n2, dev2, base2, b2, rx2, sum_send, r2r)
         steps[mark] = chain(end1, steps[mark])
         mark = len(steps)
 
+        inner = "z" if last == "y" else "y"
+        m1, _, to1 = axes[last]
+        m2, _, to2 = axes[inner]
+        g1 = HALF // m1
+        g2 = g1 // m2
+
         def own():
             end2()
-            at = rows_of(base2, n2, 0, b2, None)
-            full[k, at, :] = mine[k, at, :]
-
-        end3 = gather_steps(SMALL[second], n2, p2, dev2, base2, b2, gat_send, g2r, lambda place: None)
+            src = rows_of(base2, n2, 0, b2, None)
+            full[k, rows_of(HALF - g1, m2, 0, g2, None), :] = mine[k, src, :]
+
+        end3 = gather_steps(SMALL_G[inner], m2, to2, HALF - g1, g2, gat_send, g2r, lambda place: None)
         steps[mark] = chain(own, steps[mark])
         mark = len(steps)
 
         sends = {}
 
         def forward(event, place, half):
-            at = rows_of(0, n1, -place, b1, half)
+            at = rows_of(0, m1, -place, g1, half)
             src = full.at[k, at, pl.ds(lcol, 128)]
             return [
                 remote(src, left.at[at], fws.at[event, q - 1], fwr.at[event], c, lax.rem(x + q, NX))
-                for q in range(1, NX)
+                for q in FARX
             ]
 
         mine_to_send = jnp.logical_and(x == owner_x, lchunk == k)
@@ -331,15 +359,15 @@
                 for cp in forward(sends[place], place, None):
                     cp.start()
 
-        slots1 = slots_of(BIG[first], b1)
+        slots1 = slots_of(BIG_G[last], g1)
         counts = {}
         for a, _, _, _ in slots1:
-            key = a % n1
+            key = a % m1
             counts[key] = counts.get(key, 0) + 1
         left_over = dict(counts)
 
         def got(place):
-            key = place % n1
+            key = place % m1
             left_over[key] -= 1
             if left_over[key] == 0:
                 out(key)
@@ -348,7 +376,7 @@
             end3()
             out(0)
 
-        end4 = gather_steps(BIG[first], n1, p1, dev1, 0, b1, gat_send, g1r, got)
+        end4 = gather_steps(BIG_G[last], m1, to1, 0, g1, gat_send, g1r, got)
         steps[mark] = chain(begin, steps[mark])
         steps.append(end4)
 
@@ -367,12 +395,12 @@
             @pl.when(mine_to_get)
             def _():
                 for place, event in sends.items():
-                    at = rows_of(0, n1, -place, b1, None)
+                    at = rows_of(0, m1, -place, g1, None)
                     remote(left.at[at], left.at[at], fws.at[event, 0], fwr.at[event], c, x).wait_recv()
 
         return steps, finish, needs
 
-    plans = [[plan(k, FIRST[h]) for k in range(CHUNKS)] for h in (0, 1)]
+    plans = [[plan(k, FIRST[h], LAST[h]) for k in range(CHUNKS)] for h in (0, 1)]
 
     def comm(k, s):
         for h in (0, 1):
@@ -395,20 +423,20 @@
             folded += 1
         for k in range(CHUNKS):
             comm(k, s)
+            if s == total - 1:
+                high[k], low[k] = split(full[k])
     for u in range(units):
         push(u).wait_send()
     for k in range(CHUNKS):
         for h in (0, 1):
             pl.when(core == h)(plans[h][k][1])
 
-    lt = left[...].T
-    lhi, llo = split(lt)
+    lhi, llo = split(left[...].T)
     lhs = jnp.concatenate([lhi, llo], axis=0)
     for n in range(CHUNKS):
-        ghi, glo = split(full[n])
-        both = jnp.dot(lhs, ghi, preferred_element_type=F32)
-        low = jnp.dot(lhi, glo, preferred_element_type=F32)
-        mpart[:, n * CW : (n + 1) * CW] = both[:128] + (both[128:] + low)
+        both = jnp.dot(lhs, high[n], preferred_element_type=F32)
+        rest = jnp.dot(lhi, low[n], preferred_element_type=F32)
+        mpart[:, n * CW : (n + 1) * CW] = both[:128] + (both[128:] + rest)
     ours = pl.ds(pl.multiple_of(core * 64, 64), 64)
     other = pl.ds(pl.multiple_of((1 - core) * 64, 64), 64)
     m = remote(mpart.at[other], mrx, m_send, m_recv, sib, x)
@@ -419,9 +447,16 @@
 
 def per_device(features, coef, log_exposure, claims, cluster_id, period, period_effect):
     vmem = pl.BlockSpec(memory_space=pltpu.VMEM)
+    hbm = pl.BlockSpec(memory_space=pl.ANY)
     dma = pltpu.SemaphoreType.DMA
     chunked = pltpu.VMEM((CHUNKS, HALF, CW), F32)
     scratch = [
+        pltpu.VMEM((16, 128), F32),
+        pltpu.VMEM((16, 128), F32),
+        pltpu.VMEM((16, 128), jnp.int32),
+        pltpu.VMEM((16, 128), jnp.int32),
+        pltpu.VMEM((1, 128), F32),
+        dma((5,)),
         pltpu.VMEM((ROWS, WIDTH), BF16),
         pltpu.VMEM((16, WIDTH), BF16),
         pltpu.VMEM((NX, 16, 128), F32),
@@ -436,6 +471,8 @@
         pltpu.VMEM((HALF, 128), F32),
         pltpu.VMEM((128, WIDTH), F32),
         pltpu.VMEM((64, WIDTH), F32),
+        pltpu.VMEM((CHUNKS, HALF, CW), BF16),
+        pltpu.VMEM((CHUNKS, HALF, CW), BF16),
         dma((FCH,)),
         dma((NX - 1,)),
         dma((NX - 1,)),
@@ -447,8 +484,8 @@
     scratch += [dma((8, NX - 1)), dma((8,)), dma, dma]
     return pl.pallas_call(
         kernel,
-        out_shape=jax.ShapeDtypeStruct((64, WIDTH), F32),
-        in_specs=[pl.BlockSpec(memory_space=pl.ANY)] + [vmem] * 6,
+        out_shape=pltpu.VMEM((64, WIDTH), F32),
+        in_specs=[hbm, vmem] + [hbm] * 5,
         out_specs=vmem,
         scratch_shapes=scratch,
         compiler_params=pltpu.CompilerParams(

time: 63 us -> 61 us (0.968)
  Pallas kernels: 61.2 us -> 59.8 us
  local copies, waits for them, and re-layouts: 1.67 us -> 0.71 us
    pallas_call x1, Pallas kernels: 61.2 us -> 59.8 us  [per_device(): pl.pallas_call(kernel, out_shape=pltpu.VMEM((64, WIDTH), F32), in_specs=[...]
    unnamed x1, local copies, waits for them, and re-layouts: 1.67 us -> 0.71 us
where the time goes in v4:
time: 61 us; the launch traced here: 60.5 us
  Pallas kernels  59.8 us (98%)
  local copies, waits for them, and re-layouts  0.71 us (1%)
    pallas_call x1, Pallas kernels, per_device(): pl.pallas_call(kernel, out_shape=pltpu.VMEM((64, WIDTH), F32), in_specs=[...  59.8 us

profile of v4, /device:TPU:37, one launch (start us, length us, event | category | flops | bytes accessed | tf_op | source)
XLA Modules:
  0.0 60.5 jit_solution(16689920225108940099)
XLA Ops:
  0.0 59.8 %shard_map.73 = f32[64,1024]{1,0:T(8,128)S(1)} custom-call(bf16[2048,1024]{1,0:T(8,128)(2,1)} %feat_hbm.1, bf16[8,128]{1,0:T(8,128)(2,1)} %bitcast.10, f32[16,128]{1,0:T(8,128)} %bitcast.6, f32[16,128]{1,0:T(8,128)} %bitcast.7, s32[16,128]{1,0:T(8,128)} %bitcast.8, s32[16,128]{1,0:T(8,128)} %bitcast.9, f32[1,128]{1,0:T(1,128)} %bitcast.11), custom_call_target="tpu_custom_call" | custom-call | tf_op jit(solution)/shard_map/pallas_call | solution.py:485
  59.8 0.7 %copy.9 = f32[64,1024]{1,0:T(8,128)} copy(f32[64,1024]{1,0:T(8,128)S(1)} %shard_map.73) | data formatting | bytes 524288

commit v5 on v4

--- a/solution.py
+++ b/solution.py
@@ -30,13 +30,12 @@
 BIG = {"y": RING4, "z": RING8}
 SMALL = {"y": DIRECT4, "z": TWO8}
 FIRST = "yz"
-LAST = "zy"
+LAST = "yz"
 UNIT = 128
 EDGES = 8
 F32 = jnp.float32
 UNROLL = 4
 AHEAD = 1
-ZPEERS = (2, NZ - 2, 1, NZ - 1)
 FARX = (2, 1, 3)
 BF16 = jnp.bfloat16
 
@@ -80,14 +79,26 @@
         return (zz * NY + yy) * 2 + core
 
     barrier = pltpu.get_barrier_semaphore()
-    peers = [(cal_of(lax.rem(z + k, NZ), y), x) for k in ZPEERS]
-    peers += [(cal_of(z, lax.rem(y + k, NY)), x) for k in (2, 1, NY - 1)]
+    def greet(cal, gr):
+        pl.semaphore_signal(
+            barrier, inc=1, device_id=(cal, gr), device_id_type=pl.DeviceIdType.MESH
+        )
+
+    @pl.when(core == 0)
+    def _():
+        for k in (2, NZ - 2):
+            greet(cal_of(lax.rem(z + k, NZ), y), x)
+
+    @pl.when(core == 1)
+    def _():
+        greet(cal_of(z, lax.rem(y + 2, NY)), x)
+
+    peers = [(cal_of(lax.rem(z + k, NZ), y), x) for k in (1, NZ - 1)]
+    peers += [(cal_of(z, lax.rem(y + k, NY)), x) for k in (1, NY - 1)]
     peers += [(c, lax.rem(x + k, NX)) for k in FARX]
     peers += [(sib, x)]
     for cal, gr in peers:
-        pl.semaphore_signal(
-            barrier, inc=1, device_id=(cal, gr), device_id_type=pl.DeviceIdType.MESH
-        )
+        greet(cal, gr)
 
     small = [
         pltpu.make_async_copy(src, dst, in_sem.at[i])
@@ -125,7 +136,7 @@
             lin[x, k * (fr // 128) + j, :] = part[0, j * 128 : (j + 1) * 128]
     for f in small:
         f.wait()
-    pl.semaphore_wait(barrier, len(peers))
+    pl.semaphore_wait(barrier, len(peers) + 2 - core)
 
     for k in FARX:
         to = lax.rem(x + k, NX)

time: 61 us -> 61.3 us (level)
  no operation moved by 1% of the time
where the time goes in v5:
time: 61.3 us; the launch traced here: 60.4 us
  Pallas kernels  59.7 us (97%)
  local copies, waits for them, and re-layouts  0.71 us (1%)
    pallas_call x1, Pallas kernels, per_device(): pl.pallas_call(kernel, out_shape=pltpu.VMEM((64, WIDTH), F32), in_specs=[...  59.7 us

profile of v5, /device:TPU:37, one launch (start us, length us, event | category | flops | bytes accessed | tf_op | source)
XLA Modules:
  0.0 60.4 jit_solution(15787645667318615903)
XLA Ops:
  0.0 59.7 %shard_map.73 = f32[64,1024]{1,0:T(8,128)S(1)} custom-call(bf16[2048,1024]{1,0:T(8,128)(2,1)} %feat_hbm.1, bf16[8,128]{1,0:T(8,128)(2,1)} %bitcast.10, f32[16,128]{1,0:T(8,128)} %bitcast.6, f32[16,128]{1,0:T(8,128)} %bitcast.7, s32[16,128]{1,0:T(8,128)} %bitcast.8, s32[16,128]{1,0:T(8,128)} %bitcast.9, f32[1,128]{1,0:T(1,128)} %bitcast.11), custom_call_target="tpu_custom_call" | custom-call | tf_op jit(solution)/shard_map/pallas_call | solution.py:496
  59.7 0.7 %copy.9 = f32[64,1024]{1,0:T(8,128)} copy(f32[64,1024]{1,0:T(8,128)S(1)} %shard_map.73) | data formatting | bytes 524288
